TPU v7x, 512 devices: a whole 4x4x16 slice. The times are simulated.
512 devices in a mesh: dp: 64 (over z, y), tensor: 8 (over x, core).
Axes of the slice: x: 4, y: 4, z: 16, core: 2. Of those that a mesh axis runs over, the one named last changes fastest.
Arguments:
- query_rows: bfloat16 [24576, 3072], P('dp', 'tensor'), may hold values from -60 to 60
- key_rows: bfloat16 [24576, 3072], P('dp', 'tensor'), may hold values from -60 to 60
- value_rows: bfloat16 [24576, 3072], P('dp', 'tensor'), may hold values from -6 to 6
- kept_mask: int32 [24576], P('dp'), may hold values from 0 to 1, as said below
- block_dest: int32 [4096], P('dp'), may hold values from 0 to 63, as said below
- pack_offset: int32 [4096], P('dp'), may hold values from 0 to 319, as said below
- pack_image: int32 [20480], P('dp'), may hold values from 0 to 3, as said below
- grad_attended: bfloat16 [20480, 3072], P('dp', 'tensor'), may hold values from -18 to 18
Outputs:
- attended: bfloat16 [20480, 3072], P('dp', 'tensor')
- query_grad: bfloat16 [24576, 3072], P('dp', 'tensor')
- key_grad: bfloat16 [24576, 3072], P('dp', 'tensor')
- value_grad: bfloat16 [24576, 3072], P('dp', 'tensor')
Inputs may be any that keep to these rules, and one draw needn't show every extreme that they name: `kept_mask`: every block of 6 slots keeps at least one slot. `block_dest`: the 64 blocks of one data shard go to 64 different packs. `pack_offset`: in each pack the runs that start at these rows, with the kept counts of the blocks sent there as lengths, tile the 320 rows exactly. `pack_image`: every pack holds exactly 4 images, each one run of rows, numbered in order from 0.
All inputs are finite; a program needn't handle non-finite values.
Results may differ from a plain program's by a relative error of at most 0.0098.
Values may be sent and summed in bfloat16 or wider, within the bound.
A program may use at most 64 MiB of HBM per device.

v0:
```python
import math

import jax
import jax.numpy as jnp
from jax import lax
from jax.sharding import PartitionSpec as P

HDIM = 128
WIDTH = 3072


SOFT_LIMIT = 20.0
EPSILON = 1e-06


def local(
    query_rows, key_rows, value_rows, kept_mask, block_dest, pack_offset, pack_image, grad_attended
):
    shards = lax.axis_size("dp")
    slot_count = query_rows.shape[0]
    block_rows = slot_count // shards
    pack_rows = pack_image.shape[0]
    local_width = query_rows.shape[1]
    head_count = local_width // HDIM
    shard_line = jnp.arange(shards, dtype=jnp.int32)
    block_line = jnp.arange(block_rows, dtype=jnp.int32)
    blocks = kept_mask.reshape(shards, block_rows)
    before = jnp.cumsum(blocks, axis=1) - blocks
    matches = block_dest[:, None] == shard_line[None, :]
    owners = jnp.sum(jnp.where(matches, shard_line[:, None], 0), axis=0)
    owner_kept = jnp.take(blocks, owners, axis=0)
    owner_before = jnp.take(before, owners, axis=0)
    select = (owner_kept[:, None, :] == 1) & (owner_before[:, None, :] == block_line[None, :, None])
    position = jnp.sum(jnp.where(select, block_line[None, None, :], 0), axis=2)
    usable = jnp.any(select, axis=2).reshape(-1)
    send_rows = (owners[:, None] * block_rows + position).reshape(-1)

    def outgoing(source):
        picked = jnp.take(source, send_rows, axis=0)
        return jnp.where(usable[:, None], picked, jnp.zeros((), source.dtype)).reshape(
            shards, block_rows, local_width
        )

    pack_line = jnp.arange(pack_rows, dtype=jnp.int32)
    reached = pack_offset[None, :] <= pack_line[:, None]
    run_start = jnp.max(jnp.where(reached, pack_offset[None, :], -1), axis=1)
    sender = jnp.sum(
        jnp.where(pack_offset[None, :] == run_start[:, None], shard_line[None, :], 0), axis=1
    )
    take_rows = sender * block_rows + pack_line - run_start

    def place(received):
        return jnp.take(received.reshape(shards * block_rows, local_width), take_rows, axis=0)

    arrived = (
        lax.all_to_all(outgoing(query_rows), "dp", split_axis=0, concat_axis=0, tiled=True),
        lax.all_to_all(outgoing(key_rows), "dp", split_axis=0, concat_axis=0, tiled=True),
        lax.all_to_all(outgoing(value_rows), "dp", split_axis=0, concat_axis=0, tiled=True),
    )
    packed_query = place(arrived[0])
    packed_key = place(arrived[1])
    packed_value = place(arrived[2])
    query_float = packed_query.astype(jnp.float32)
    key_float = packed_key.astype(jnp.float32)
    totals = lax.psum(
        (jnp.sum(query_float * query_float, axis=1), jnp.sum(key_float * key_float, axis=1)),
        "tensor",
    )
    scale_query = 1.0 / jnp.sqrt(totals[0] / WIDTH + EPSILON)
    scale_key = 1.0 / jnp.sqrt(totals[1] / WIDTH + EPSILON)
    normed_query = query_float * scale_query[:, None]
    normed_key = key_float * scale_key[:, None]
    round_query = normed_query.astype(jnp.bfloat16).reshape(pack_rows, head_count, HDIM)
    round_key = normed_key.astype(jnp.bfloat16).reshape(pack_rows, head_count, HDIM)
    value_heads = packed_value.reshape(pack_rows, head_count, HDIM)
    raw_scores = jnp.einsum(
        "qhd,khd->hqk", round_query, round_key, preferred_element_type=jnp.float32
    ) / math.sqrt(HDIM)
    capped = SOFT_LIMIT * jnp.tanh(raw_scores / SOFT_LIMIT)
    same_image = (pack_image[:, None] == pack_image[None, :]).astype(jnp.float32)
    weight = jnp.exp(capped) * same_image[None]
    attention = weight / jnp.sum(weight, axis=2, keepdims=True)
    round_probs = attention.astype(jnp.bfloat16)
    attended = jnp.einsum(
        "hqk,khd->qhd", round_probs, value_heads, preferred_element_type=jnp.float32
    )
    attended = attended.astype(jnp.bfloat16).reshape(pack_rows, local_width)
    cotangent = grad_attended.reshape(pack_rows, head_count, HDIM)
    value_back = jnp.einsum(
        "hqk,qhd->khd", round_probs, cotangent, preferred_element_type=jnp.float32
    )
    value_back = value_back.astype(jnp.bfloat16).reshape(pack_rows, local_width)
    return_rows = jnp.minimum(pack_offset[:, None] + block_line[None, :], pack_rows - 1).reshape(-1)

    def outbound(source):
        return jnp.take(source, return_rows, axis=0).reshape(shards, block_rows, local_width)

    prob_grad = jnp.einsum(
        "qhd,khd->hqk", cotangent, value_heads, preferred_element_type=jnp.float32
    )
    score_grad = (
        attention
        * (prob_grad - jnp.sum(attention * prob_grad, axis=2, keepdims=True))
        * (1.0 - (capped / SOFT_LIMIT) ** 2)
        / math.sqrt(HDIM)
    )
    round_grad = score_grad.astype(jnp.bfloat16)
    normed_query_grad = jnp.einsum(
        "hqk,khd->qhd", round_grad, round_key, preferred_element_type=jnp.float32
    ).reshape(pack_rows, local_width)
    normed_key_grad = jnp.einsum(
        "hqk,qhd->khd", round_grad, round_query, preferred_element_type=jnp.float32
    ).reshape(pack_rows, local_width)
    inner = lax.psum(
        (
            jnp.sum(normed_query_grad * normed_query, axis=1),
            jnp.sum(normed_key_grad * normed_key, axis=1),
        ),
        "tensor",
    )
    query_back = (
        scale_query[:, None] * (normed_query_grad - normed_query * (inner[0] / WIDTH)[:, None])
    ).astype(jnp.bfloat16)
    key_back = (
        scale_key[:, None] * (normed_key_grad - normed_key * (inner[1] / WIDTH)[:, None])
    ).astype(jnp.bfloat16)
    query_home, key_home, value_home = (
        lax.all_to_all(outbound(query_back), "dp", split_axis=0, concat_axis=0, tiled=True),
        lax.all_to_all(outbound(key_back), "dp", split_axis=0, concat_axis=0, tiled=True),
        lax.all_to_all(outbound(value_back), "dp", split_axis=0, concat_axis=0, tiled=True),
    )
    home_rows = (block_dest[:, None] * block_rows + before).reshape(-1)
    kept_rows = kept_mask[:, None] == 1

    def unpack(received):
        flat = received.reshape(shards * block_rows, local_width)
        return jnp.where(kept_rows, jnp.take(flat, home_rows, axis=0), jnp.zeros((), jnp.bfloat16))

    return (attended, unpack(query_home), unpack(key_home), unpack(value_home))


def solution(mesh):
    in_specs = (
        P("dp", "tensor"),
        P("dp", "tensor"),
        P("dp", "tensor"),
        P("dp"),
        P("dp"),
        P("dp"),
        P("dp"),
        P("dp", "tensor"),
    )
    out_specs = (P("dp", "tensor"), P("dp", "tensor"), P("dp", "tensor"), P("dp", "tensor"))
    return jax.shard_map(local, mesh=mesh, in_specs=in_specs, out_specs=out_specs, check_vma=False)
```

profile of v0, /device:TPU:1, one launch (start us, length us, event | category | flops | bytes accessed | tf_op | source)
XLA Modules:
  0.0 273.5 jit_solution(17304209605094496291)
XLA Ops:
  0.6 0.8 select_reduce_fusion.2
  1.5 0.8 reshape.154
  2.5 0.6 gather_fusion
  3.2 0.6 gather_fusion.1
  4.6 2.1 gather_fusion.6
  6.7 2.1 gather_fusion.4
  8.9 2.1 gather_fusion.2
  11.3 0.8 reshape.158
  12.1 19.4 %all-to-all-start.1 = ((bf16[64,6,384]{2,1,0:T(8,128)(2,1)}), bf16[64,6,384]{2,1,0:T(8,128)(2,1)S(1)}, u32[]{:S(2)}, u32[]{:S(2)}) async-start(bf16[64,6,384]{2,1,0:T(8,128)(2,1)} %reshape.158), calls=%async_computation.1 | async-start | bytes 786432 | tf_op jit(solution)/shard_map/all_to_all | solution.py:56
  31.5 0.8 reshape.161
  32.4 24.1 %all-to-all-done.1 = bf16[64,6,384]{2,1,0:T(8,128)(2,1)S(1)} async-done(((bf16[64,6,384]{2,1,0:T(8,128)(2,1)}), bf16[64,6,384]{2,1,0:T(8,128)(2,1)S(1)}, u32[]{:S(2)}, u32[]{:S(2)}) %all-to-all-start.1) | async-done | bytes 294944 | tf_op jit(solution)/shard_map/all_to_all | solution.py:56
  56.4 7.5 %all-to-all-start.2 = ((bf16[64,6,384]{2,1,0:T(8,128)(2,1)}), bf16[64,6,384]{2,1,0:T(8,128)(2,1)S(1)}, u32[]{:S(2)}, u32[]{:S(2)}) async-start(bf16[64,6,384]{2,1,0:T(8,128)(2,1)} %reshape.161), calls=%async_computation.2 | async-start | bytes 786432 | tf_op jit(solution)/shard_map/all_to_all | solution.py:57
  63.9 0.8 reshape.155
  64.9 22.7 %all-to-all-done.2 = bf16[64,6,384]{2,1,0:T(8,128)(2,1)S(1)} async-done(((bf16[64,6,384]{2,1,0:T(8,128)(2,1)}), bf16[64,6,384]{2,1,0:T(8,128)(2,1)S(1)}, u32[]{:S(2)}, u32[]{:S(2)}) %all-to-all-start.2) | async-done | bytes 294944 | tf_op jit(solution)/shard_map/all_to_all | solution.py:57
  87.6 8.8 %all-to-all-start = ((bf16[64,6,384]{2,1,0:T(8,128)(2,1)}), bf16[64,6,384]{2,1,0:T(8,128)(2,1)S(1)}, u32[]{:S(2)}, u32[]{:S(2)}) async-start(bf16[64,6,384]{2,1,0:T(8,128)(2,1)} %reshape.155), calls=%async_computation | async-start | bytes 786432 | tf_op jit(solution)/shard_map/all_to_all | solution.py:58
  97.7 2.0 gather_fusion.5
  99.8 2.0 gather_fusion.7
  101.9 18.1 %all-to-all-done = bf16[64,6,384]{2,1,0:T(8,128)(2,1)S(1)} async-done(((bf16[64,6,384]{2,1,0:T(8,128)(2,1)}), bf16[64,6,384]{2,1,0:T(8,128)(2,1)S(1)}, u32[]{:S(2)}, u32[]{:S(2)}) %all-to-all-start) | async-done | bytes 294944 | tf_op jit(solution)/shard_map/all_to_all | solution.py:58
  120.1 2.0 gather_fusion.3
  122.9 17.0 %all-reduce.1 = (f32[320]{0:T(512)S(1)}, f32[320]{0:T(512)S(1)}) all-reduce(f32[320]{0:T(512)S(1)} %get-tuple-element.23, f32[320]{0:T(512)S(1)} %get-tuple-element.22), channel_id=1, replica_groups=mesh['dp'=64,'tensor'=8] {'tensor'}, use_global_device_ids=true, to_apply=%region_7.11 | all-reduce | flops 640 | bytes 5120 | tf_op jit(solution)/shard_map/psum | solution.py:65
  140.3 0.9 copy.79
  141.2 1.5 fusion.44
  142.8 0.6 fusion.6
  143.4 1.2 fusion.8
  144.6 3.8 %convolution_bitcast_fusion.1 = f32[320,3,128]{2,0,1:T(8,128)} fusion(bf16[320,3,128]{0,2,1:T(8,128)(2,1)S(1)} %bitcast.54, f32[3,320,320]{2,1,0:T(8,128)} %fusion.44, f32[3,320,320]{1,2,0:T(8,128)S(1)} %get-tuple-element.49, f32[3,320]{1,0:T(4,128)S(1)} %get-tuple-element.48, f32[320,320]{0,1:T(8,128)S(1)} %compare_convert_fusion), kind=kOutput, calls=%fused_computation.24 | convolution fusion | flops 82945280 | bytes 3608320 | tf_op jit(solution)/shard_map/hqk,khd->qhd/dot_general | solution.py:108
  148.4 2.9 %convolution_bitcast_fusion = f32[320,3,128]{2,0,1:T(8,128)S(1)} fusion(bf16[320,3,128]{0,2,1:T(8,128)(2,1)S(1)} %bitcast.56, f32[3,320,320]{2,1,0:T(8,128)} %fusion.44, f32[3,320,320]{1,2,0:T(8,128)S(1)} %get-tuple-element.49, f32[3,320]{1,0:T(4,128)} %copy-done.13, f32[320,320]{0,1:T(8,128)S(1)} %compare_convert_fusion), kind=kOutput, calls=%fused_computation.23 | convolution fusion | flops 82945280 | bytes 3608320 | tf_op jit(solution)/shard_map/hqk,qhd->khd/dot_general | solution.py:111
  151.3 1.2 copy.99
  153.1 1.3 copy.91
  154.9 12.4 %all-reduce = (f32[320]{0:T(512)S(1)}, f32[320]{0:T(512)S(1)}) all-reduce(f32[320]{0:T(512)S(1)} %get-tuple-element.21, f32[320]{0:T(512)S(1)} %get-tuple-element.20), channel_id=1, replica_groups=mesh['dp'=64,'tensor'=8] {'tensor'}, use_global_device_ids=true, to_apply=%region_13.17 | all-reduce | flops 640 | bytes 5120 | tf_op jit(solution)/shard_map/psum | solution.py:114
  167.3 2.1 gather_fusion.12
  169.8 2.1 gather_fusion.10
  172.0 2.1 gather_fusion.8
  174.3 0.8 reshape.173
  175.1 6.6 %all-to-all-start.5 = ((bf16[64,6,384]{2,1,0:T(8,128)(2,1)}), bf16[64,6,384]{2,1,0:T(8,128)(2,1)S(1)}, u32[]{:S(2)}, u32[]{:S(2)}) async-start(bf16[64,6,384]{2,1,0:T(8,128)(2,1)} %reshape.173), calls=%async_computation.5 | async-start | bytes 786432 | tf_op jit(solution)/shard_map/all_to_all | solution.py:130
  181.8 0.8 reshape.170
  182.6 23.9 %all-to-all-done.5 = bf16[64,6,384]{2,1,0:T(8,128)(2,1)S(1)} async-done(((bf16[64,6,384]{2,1,0:T(8,128)(2,1)}), bf16[64,6,384]{2,1,0:T(8,128)(2,1)S(1)}, u32[]{:S(2)}, u32[]{:S(2)}) %all-to-all-start.5) | async-done | bytes 294944 | tf_op jit(solution)/shard_map/all_to_all | solution.py:130
  206.5 7.6 %all-to-all-start.4 = ((bf16[64,6,384]{2,1,0:T(8,128)(2,1)}), bf16[64,6,384]{2,1,0:T(8,128)(2,1)S(1)}, u32[]{:S(2)}, u32[]{:S(2)}) async-start(bf16[64,6,384]{2,1,0:T(8,128)(2,1)} %reshape.170), calls=%async_computation.4 | async-start | bytes 786432 | tf_op jit(solution)/shard_map/all_to_all | solution.py:129
  214.1 0.8 reshape.167
  215.0 22.8 %all-to-all-done.4 = bf16[64,6,384]{2,1,0:T(8,128)(2,1)S(1)} async-done(((bf16[64,6,384]{2,1,0:T(8,128)(2,1)}), bf16[64,6,384]{2,1,0:T(8,128)(2,1)S(1)}, u32[]{:S(2)}, u32[]{:S(2)}) %all-to-all-start.4) | async-done | bytes 294944 | tf_op jit(solution)/shard_map/all_to_all | solution.py:129
  237.8 9.0 %all-to-all-start.3 = ((bf16[64,6,384]{2,1,0:T(8,128)(2,1)}), bf16[64,6,384]{2,1,0:T(8,128)(2,1)S(1)}, u32[]{:S(2)}, u32[]{:S(2)}) async-start(bf16[64,6,384]{2,1,0:T(8,128)(2,1)} %reshape.167), calls=%async_computation.3 | async-start | bytes 786432 | tf_op jit(solution)/shard_map/all_to_all | solution.py:128
  247.2 2.2 fusion.7
  249.4 1.1 copy.85
  250.6 0.9 copy.101
  251.5 2.1 gather_fusion.13
  253.8 2.1 gather_fusion.11
  255.9 14.2 %all-to-all-done.3 = bf16[64,6,384]{2,1,0:T(8,128)(2,1)S(1)} async-done(((bf16[64,6,384]{2,1,0:T(8,128)(2,1)}), bf16[64,6,384]{2,1,0:T(8,128)(2,1)S(1)}, u32[]{:S(2)}, u32[]{:S(2)}) %all-to-all-start.3) | async-done | bytes 294944 | tf_op jit(solution)/shard_map/all_to_all | solution.py:128
  270.2 2.1 gather_fusion.9
  272.3 1.1 select_select_fusion
  (94 shorter events, 6.5 us)
Async XLA Ops:
  0.6 3.9 %copy-start = (bf16[384,384]{1,0:T(8,128)(2,1)S(1)}, bf16[384,384]{1,0:T(8,128)(2,1)}, u32[]{:S(2)}) copy-start(bf16[384,384]{1,0:T(8,128)(2,1)} %param.17) | copy-start | bytes 884740
  2.5 0.7 copy-start.8
  3.8 2.9 %copy-start.1 = (bf16[384,384]{1,0:T(8,128)(2,1)S(1)}, bf16[384,384]{1,0:T(8,128)(2,1)}, u32[]{:S(2)}) copy-start(bf16[384,384]{1,0:T(8,128)(2,1)} %param.16) | copy-start | bytes 884740
  6.7 2.2 copy-start.2
  12.1 52.6 %copy-start.15 = (s32[64]{0:T(128)S(1)}, s32[64]{0:T(128)}, u32[]{:S(2)}) copy-start(s32[64]{0:T(128)} %param.21) | copy-start | bytes 772
  12.1 44.3 %all-to-all-start.1 = ((bf16[64,6,384]{2,1,0:T(8,128)(2,1)}), bf16[64,6,384]{2,1,0:T(8,128)(2,1)S(1)}, u32[]{:S(2)}, u32[]{:S(2)}) async-start(bf16[64,6,384]{2,1,0:T(8,128)(2,1)} %reshape.158), calls=%async_computation.1 | async-start | bytes 786432 | tf_op jit(solution)/shard_map/all_to_all | solution.py:56
  31.5 65.1 %copy-start.10 = (bf16[320,384]{1,0:T(8,128)(2,1)S(1)}, bf16[320,384]{1,0:T(8,128)(2,1)}, u32[]{:S(2)}) copy-start(bf16[320,384]{1,0:T(8,128)(2,1)} %param.23) | copy-start | bytes 737284
  32.4 65.1 %copy-start.11 = (s32[320]{0:T(512)S(1)}, s32[320]{0:T(512)}, u32[]{:S(2)}) copy-start(s32[320]{0:T(512)} %param.22) | copy-start | bytes 3844
  56.4 31.1 %all-to-all-start.2 = ((bf16[64,6,384]{2,1,0:T(8,128)(2,1)}), bf16[64,6,384]{2,1,0:T(8,128)(2,1)S(1)}, u32[]{:S(2)}, u32[]{:S(2)}) async-start(bf16[64,6,384]{2,1,0:T(8,128)(2,1)} %reshape.161), calls=%async_computation.2 | async-start | bytes 786432 | tf_op jit(solution)/shard_map/all_to_all | solution.py:57
  87.6 32.4 %all-to-all-start = ((bf16[64,6,384]{2,1,0:T(8,128)(2,1)}), bf16[64,6,384]{2,1,0:T(8,128)(2,1)S(1)}, u32[]{:S(2)}, u32[]{:S(2)}) async-start(bf16[64,6,384]{2,1,0:T(8,128)(2,1)} %reshape.155), calls=%async_computation | async-start | bytes 786432 | tf_op jit(solution)/shard_map/all_to_all | solution.py:58
  122.5 20.2 %copy-start.5 = (bf16[320,384]{0,1:T(8,128)(2,1)}, bf16[320,384]{0,1:T(8,128)(2,1)S(1)}, u32[]{:S(2)}) copy-start(bf16[320,384]{0,1:T(8,128)(2,1)S(1)} %copy.78) | copy-start | bytes 737284
  141.2 1.5 copy-start.6
  143.4 1.2 copy-start.13
  143.4 5.0 %copy-start.3 = (f32[3,320,320]{1,2,0:T(8,128)}, f32[3,320,320]{1,2,0:T(8,128)S(1)}, u32[]{:S(2)}) copy-start(f32[3,320,320]{1,2,0:T(8,128)S(1)} %get-tuple-element.49) | copy-start | bytes 3686404
  144.6 3.8 %copy-start.7 = (bf16[320,384]{0,1:T(8,128)(2,1)S(1)}, bf16[320,384]{0,1:T(8,128)(2,1)}, u32[]{:S(2)}) copy-start(bf16[320,384]{0,1:T(8,128)(2,1)} %copy.79) | copy-start | bytes 737284
  172.0 2.2 copy-start.16
  175.1 31.4 %all-to-all-start.5 = ((bf16[64,6,384]{2,1,0:T(8,128)(2,1)}), bf16[64,6,384]{2,1,0:T(8,128)(2,1)S(1)}, u32[]{:S(2)}, u32[]{:S(2)}) async-start(bf16[64,6,384]{2,1,0:T(8,128)(2,1)} %reshape.173), calls=%async_computation.5 | async-start | bytes 786432 | tf_op jit(solution)/shard_map/all_to_all | solution.py:130
  181.7 65.1 %copy-start.9 = (s32[64,6]{1,0:T(8,128)S(1)}, s32[64,6]{1,0:T(8,128)}, u32[]{:S(2)}) copy-start(s32[64,6]{1,0:T(8,128)} %copy-done.8) | copy-start | bytes 4612
  181.7 65.2 %copy-start.17 = (s32[64]{0:T(128)S(1)}, s32[64]{0:T(128)}, u32[]{:S(2)}) copy-start(s32[64]{0:T(128)} %param.20) | copy-start | bytes 772
  181.8 65.4 %copy-start.12 = (s32[384]{0:T(512)S(1)}, s32[384]{0:T(512)}, u32[]{:S(2)}) copy-start(s32[384]{0:T(512)} %param.19) | copy-start | bytes 4612
  181.8 65.5 %copy-start.4 = (f32[3,320,320]{1,2,0:T(8,128)S(1)}, f32[3,320,320]{1,2,0:T(8,128)}, u32[]{:S(2)}) copy-start(f32[3,320,320]{1,2,0:T(8,128)} %copy-done.3) | copy-start | bytes 3686404
  181.8 65.5 %copy-start.14 = (f32[3,320]{1,0:T(4,128)S(1)}, f32[3,320]{1,0:T(4,128)}, u32[]{:S(2)}) copy-start(f32[3,320]{1,0:T(4,128)} %copy-done.13) | copy-start | bytes 11524
  206.5 31.2 %all-to-all-start.4 = ((bf16[64,6,384]{2,1,0:T(8,128)(2,1)}), bf16[64,6,384]{2,1,0:T(8,128)(2,1)S(1)}, u32[]{:S(2)}, u32[]{:S(2)}) async-start(bf16[64,6,384]{2,1,0:T(8,128)(2,1)} %reshape.170), calls=%async_computation.4 | async-start | bytes 786432 | tf_op jit(solution)/shard_map/all_to_all | solution.py:129
  237.8 32.3 %all-to-all-start.3 = ((bf16[64,6,384]{2,1,0:T(8,128)(2,1)}), bf16[64,6,384]{2,1,0:T(8,128)(2,1)S(1)}, u32[]{:S(2)}, u32[]{:S(2)}) async-start(bf16[64,6,384]{2,1,0:T(8,128)(2,1)} %reshape.167), calls=%async_computation.3 | async-start | bytes 786432 | tf_op jit(solution)/shard_map/all_to_all | solution.py:128
where the time goes:
time: 277 us; the launch traced here: 273 us
  waiting for transfers between devices  126 us (45%)
  starting transfers between devices  58.8 us (21%)
  local copies, waits for them, and re-layouts  41.1 us (15%)
  blocking collectives  29.4 us (11%)
  matrix products  12.2 us (4%)
  other arithmetic  5.06 us (2%)
    all_to_all x1, waiting for transfers between devices, local(): lax.all_to_all(outgoing(query_rows), 'dp', split_axis=0, concat_axis=0, t...  24.1 us
    all_to_all x1, waiting for transfers between devices, local(): lax.all_to_all(outbound(value_back), 'dp', split_axis=0, concat_axis=0, t...  23.9 us
    all_to_all x1, waiting for transfers between devices, local(): lax.all_to_all(outbound(key_back), 'dp', split_axis=0, concat_axis=0, til...  22.8 us
    all_to_all x1, waiting for transfers between devices, local(): lax.all_to_all(outgoing(key_rows), 'dp', split_axis=0, concat_axis=0, til...  22.7 us
    all_to_all x1, starting transfers between devices, local(): lax.all_to_all(outgoing(query_rows), 'dp', split_axis=0, concat_axis=0, t...  19.4 us
    all_to_all x1, waiting for transfers between devices, local(): lax.all_to_all(outgoing(value_rows), 'dp', split_axis=0, concat_axis=0, t...  18.1 us
    psum x1, blocking collectives, local(): lax.psum((jnp.sum(query_float * query_float, axis=1), jnp.sum(key_float *...  17 us
    all_to_all x1, waiting for transfers between devices, local(): lax.all_to_all(outbound(query_back), 'dp', split_axis=0, concat_axis=0, t...  14.2 us
  transfers between devices with their start and end apart: 6, of which 6 were waited for; matrix products, arithmetic and copies ran while one was open for 7% of the time, Pallas kernels for 0%

commit v1 on v0

v1 whole, which is shorter than its diff:
```python
import math

import jax
import jax.numpy as jnp
from jax import lax
from jax.experimental import pallas as pl
from jax.experimental.pallas import tpu as pltpu
from jax.sharding import PartitionSpec as P

HDIM = 128
WIDTH = 3072
SOFT_LIMIT = 20.0
EPSILON = 1e-06

MESH = pl.DeviceIdType.MESH
BF = jnp.bfloat16
F32 = jnp.float32
I32 = jnp.int32

NZ = 16
NY = 4
SHARDS = NZ * NY
BLOCK = 6
SLOTS = SHARDS * BLOCK
PACK = 320
COLS = 384
HEADS = COLS // HDIM
LANES = 384
TENSOR = 8

Q, K, V, DV, DQ, DK = range(6)


def mm(a, b):
    return lax.dot_general(a, b, (((1,), (0,)), ((), ())), preferred_element_type=F32)


def mm_nt(a, b):
    return lax.dot_general(a, b, (((1,), (1,)), ((), ())), preferred_element_type=F32)


def mm_tn(a, b):
    return lax.dot_general(a, b, (((0,), (0,)), ((), ())), preferred_element_type=F32)


def iota(shape, dim):
    return lax.broadcasted_iota(I32, shape, dim)


def sixth(x):
    return (x * 10923) >> 16


def one_hot(row, rows):
    return jnp.where(iota((rows, row.shape[1]), 0) == row, 1.0, 0.0).astype(BF)


def row_sums(product):
    high = product.astype(BF)
    low = (product - high.astype(F32)).astype(BF)
    ones = jnp.ones((8, COLS), BF)
    return mm_nt(ones, high) + mm_nt(ones, low)


def column(row):
    return jnp.transpose(jnp.broadcast_to(row, (128, LANES)))[:PACK, 0:1]


def kernel(
    kept_ref, dest_ref, offset_ref, image_ref, q_hbm, k_hbm, v_hbm, g_hbm,
    att_ref, dq_ref, dk_ref, dv_ref,
    qkv, cot, ysend, yrecv, zsend, zrecv, xsend, xrecv,
    gather_y, unpack, place, place_y, back_y, regroup, regroup_inv,
    probs, tanhs, packed_q, packed_k, normed_q, normed_k, grad_q, grad_k,
    load_sem, ysend_sem, yrecv_sem, zsend_sem, zrecv_sem, xsend_sem, xrecv_sem,
):
    dp = lax.axis_index("dp")
    tensor = lax.axis_index("tensor")
    z, y = dp // NY, dp % NY

    def y_peer(i):
        return lax.rem(y + i + 1, NY)

    def z_peer(i):
        half = (i + 1) // 2 + (i + 1) % 2
        return lax.rem(z + jnp.where(i % 2 == 0, half, NZ - half), NZ)

    def x_peer(i):
        return lax.rem(tensor + i + 1, TENSOR)

    barrier = pltpu.get_barrier_semaphore()

    def greet_z(i, carry):
        pl.semaphore_signal(
            barrier, inc=1, device_id={"dp": z_peer(i) * NY + y}, device_id_type=MESH
        )
        return carry

    def greet_y(i, carry):
        pl.semaphore_signal(
            barrier, inc=1, device_id={"dp": z * NY + y_peer(i)}, device_id_type=MESH
        )
        return carry

    def greet_x(i, carry):
        pl.semaphore_signal(barrier, inc=1, device_id={"tensor": x_peer(i)}, device_id_type=MESH)
        return carry

    lax.fori_loop(0, NZ - 1, greet_z, 0)
    lax.fori_loop(0, NY - 1, greet_y, 0)
    lax.fori_loop(0, TENSOR - 1, greet_x, 0)

    loads = [
        pltpu.make_async_copy(source, target, load_sem.at[i])
        for i, (source, target) in enumerate(
            ((q_hbm, qkv.at[0]), (k_hbm, qkv.at[1]), (v_hbm, qkv.at[2]), (g_hbm, cot))
        )
    ]
    for load in loads:
        load.start()

    def send_y(array):
        def one(i, carry):
            peer = y_peer(i)
            pltpu.make_async_remote_copy(
                ysend.at[array, peer], yrecv.at[array, y], ysend_sem.at[array], yrecv_sem.at[array],
                device_id={"dp": z * NY + peer}, device_id_type=MESH,
            ).start()
            return carry

        lax.fori_loop(0, NY - 1, one, 0)
        yrecv[array, y] = ysend[array, y]

    def wait_y(array):
        part = yrecv.at[array, pl.ds(0, NY - 1)]
        pltpu.make_async_copy(part, part, yrecv_sem.at[array]).wait()
        return yrecv[array].reshape(SLOTS, COLS)

    def send_z(array):
        def one(i, carry):
            peer = z_peer(i)
            pltpu.make_async_remote_copy(
                zsend.at[array, peer], zrecv.at[array, z], zsend_sem.at[array], zrecv_sem.at[array],
                device_id={"dp": peer * NY + y}, device_id_type=MESH,
            ).start()
            return carry

        lax.fori_loop(0, NZ - 1, one, 0)
        zrecv[array, z] = zsend[array, z]

    def wait_z(array):
        part = zrecv.at[array, pl.ds(0, NZ - 1)]
        pltpu.make_async_copy(part, part, zrecv_sem.at[array]).wait()
        return zrecv[array].reshape(SLOTS, COLS)

    def send_x(which):
        def one(i, carry):
            peer = x_peer(i)
            pltpu.make_async_remote_copy(
                xsend.at[which], xrecv.at[which, tensor], xsend_sem.at[which], xrecv_sem.at[which],
                device_id={"tensor": peer}, device_id_type=MESH,
            ).start()
            return carry

        lax.fori_loop(0, TENSOR - 1, one, 0)
        xrecv[which, tensor] = xsend[which]

    def wait_x(which):
        part = xrecv.at[which, pl.ds(0, TENSOR - 1)]
        pltpu.make_async_copy(part, part, xrecv_sem.at[which]).wait()
        return jnp.sum(xrecv[which], axis=0)

    def put_y(array, rows):
        ysend[array] = rows.astype(BF).reshape(NY, SLOTS // NY, COLS)

    def put_z(array, rows):
        zsend[array] = rows.astype(BF).reshape(NZ, SLOTS // NZ, COLS)

    line = iota((1, SLOTS), 1)
    unit = sixth(line)
    spot = line - BLOCK * unit
    unit_y = (unit & (NZ - 1)) * NY + (unit >> 4)
    down = iota((SLOTS, SLOTS), 0)
    across = iota((SLOTS, SLOTS), 1)
    earlier = jnp.where((sixth(down) == sixth(across)) & (down < across), 1.0, 0.0).astype(BF)
    kept = kept_ref[...]
    before = mm(jnp.broadcast_to(kept.astype(F32), (8, SLOTS)).astype(BF), earlier)[0:1]
    before = before.astype(I32)
    which = iota((8, SHARDS), 0)
    dest = dest_ref[...]
    offset = offset_ref[...]
    parts = jnp.where(which == 0, dest, jnp.where(which == 1, offset >> 4, offset & 15))
    parts = parts.astype(F32).astype(BF)
    spread = mm(parts, one_hot(unit, SHARDS)).astype(I32)
    spread_y = mm(parts, one_hot(unit_y, SHARDS)).astype(I32)
    dest_slot = spread[0:1]
    first = spread[1:2] * 16 + spread[2:3]
    first_y = spread_y[1:2] * 16 + spread_y[2:3]
    dest_y = (dest_slot & (NY - 1)) * NZ + (dest_slot >> 2)
    target = jnp.where(kept == 1, dest_slot * BLOCK + before, -1)
    target_y = jnp.where(kept == 1, dest_y * BLOCK + before, -1)

    gather = one_hot(target, SLOTS)
    loads[0].wait()
    put_z(Q, mm(gather, qkv[0]))
    pl.semaphore_wait(barrier, (NZ - 1) + (NY - 1) + (TENSOR - 1))
    send_z(Q)

    gather_y[...] = one_hot(target_y, SLOTS)
    loads[1].wait()
    put_y(K, mm(gather_y[...], qkv[1]))
    send_y(K)
    loads[2].wait()
    put_y(V, mm(gather_y[...], qkv[2]))
    send_y(V)

    identity = jnp.where(down == across, 1.0, 0.0).astype(BF)
    regroup[...] = one_hot(unit_y * BLOCK + spot, SLOTS)
    put_z(K, mm(regroup[...], wait_y(K)))
    send_z(K)
    put_z(V, mm(regroup[...], wait_y(V)))
    send_z(V)

    unpack[...] = mm_nt(identity, gather).astype(BF)
    place[...] = one_hot(first + spot, PACK)
    place_y[...] = one_hot(first_y + spot, PACK)
    back_y[...] = mm_nt(identity, place_y[...]).astype(BF)
    unit_n = (unit & (NY - 1)) * NZ + (unit >> 2)
    regroup_inv[...] = one_hot(unit_n * BLOCK + spot, SLOTS)

    image = jnp.broadcast_to(image_ref[...], (8, PACK))
    image_hot = jnp.where(image == iota((8, PACK), 0), 1.0, 0.0).astype(BF)
    same = mm_tn(image_hot, image_hot)

    xsend[...] = jnp.zeros((3, 8, LANES), F32)

    put_y(Q, mm(regroup_inv[...], wait_z(Q)))
    send_y(Q)
    packed = mm(place_y[...], wait_y(Q))
    packed_q[...] = packed
    xsend[0, :, :PACK] = row_sums(packed * packed)
    send_x(0)

    packed = mm(place[...], wait_z(K))
    packed_k[...] = packed
    xsend[1, :, :PACK] = row_sums(packed * packed)
    send_x(1)

    scale_q = column(lax.rsqrt(wait_x(0)[0:1] / WIDTH + EPSILON))
    packed_q[...] = packed_q[...] * scale_q
    normed_q[...] = packed_q[...].astype(BF)
    scale_k = column(lax.rsqrt(wait_x(1)[0:1] / WIDTH + EPSILON))
    packed_k[...] = packed_k[...] * scale_k
    normed_k[...] = packed_k[...].astype(BF)

    loads[3].wait()
    value_back = []
    for h in range(HEADS):
        cols = slice(h * HDIM, (h + 1) * HDIM)
        raw = mm_nt(normed_q[:, cols], normed_k[:, cols]) / math.sqrt(HDIM)
        bent = jnp.tanh(raw / SOFT_LIMIT)
        weight = jnp.exp(SOFT_LIMIT * bent) * same
        prob = weight / jnp.sum(weight, axis=1, keepdims=True)
        probs[h] = prob
        tanhs[h] = bent
        value_back.append(mm_tn(prob.astype(BF), cot[:, cols]).astype(BF))
    put_y(DV, mm(back_y[...], jnp.concatenate(value_back, axis=1)))
    send_y(DV)
    put_z(DV, mm(regroup[...], wait_y(DV)))
    send_z(DV)

    value = mm(place[...], wait_z(V)).astype(BF)
    for h in range(HEADS):
        cols = slice(h * HDIM, (h + 1) * HDIM)
        prob = probs[h]
        bent = tanhs[h]
        prob_grad = mm_nt(cot[:, cols], value[:, cols])
        inner = jnp.sum(prob * prob_grad, axis=1, keepdims=True)
        score = prob * (prob_grad - inner) * (1.0 - bent * bent) / math.sqrt(HDIM)
        score = score.astype(BF)
        grad_q[:, cols] = mm(score, normed_k[:, cols])
        grad_k[:, cols] = mm_tn(score, normed_q[:, cols])
    sums_q = row_sums(grad_q[...] * packed_q[...])
    sums_k = row_sums(grad_k[...] * packed_k[...])
    xsend[2, :, :PACK] = jnp.where(iota((8, PACK), 0) == 0, sums_q, sums_k)
    send_x(2)
    for h in range(HEADS):
        cols = slice(h * HDIM, (h + 1) * HDIM)
        att_ref[:, cols] = mm(probs[h].astype(BF), value[:, cols]).astype(BF)
    inner = wait_x(2) / WIDTH
    back = scale_q * (grad_q[...] - packed_q[...] * column(inner[0:1]))
    put_y(DQ, mm(back_y[...], back.astype(BF)))
    send_y(DQ)
    back = scale_k * (grad_k[...] - packed_k[...] * column(inner[1:2]))
    put_y(DK, mm(back_y[...], back.astype(BF)))
    send_y(DK)
    put_z(DQ, mm(regroup[...], wait_y(DQ)))
    send_z(DQ)
    put_z(DK, mm(regroup[...], wait_y(DK)))
    send_z(DK)

    dv_ref[...] = mm(unpack[...], wait_z(DV)).astype(BF)
    dq_ref[...] = mm(unpack[...], wait_z(DQ)).astype(BF)
    dk_ref[...] = mm(unpack[...], wait_z(DK)).astype(BF)

    for array in range(6):
        part = ysend.at[array, pl.ds(0, NY - 1)]
        pltpu.make_async_copy(part, part, ysend_sem.at[array]).wait()
        part = zsend.at[array, pl.ds(0, NZ - 1)]
        pltpu.make_async_copy(part, part, zsend_sem.at[array]).wait()
    for which in range(3):
        part = xrecv.at[which, pl.ds(0, TENSOR - 1)]
        pltpu.make_async_copy(part, part, xsend_sem.at[which]).wait()


def local(
    query_rows, key_rows, value_rows, kept_mask, block_dest, pack_offset, pack_image, grad_attended
):
    vmem = pl.BlockSpec(memory_space=pltpu.VMEM)
    hbm = pl.BlockSpec(memory_space=pl.ANY)
    dma = pltpu.SemaphoreType.DMA
    slots = jax.ShapeDtypeStruct((SLOTS, COLS), BF)
    square = pltpu.VMEM((SLOTS, SLOTS), BF)
    return pl.pallas_call(
        kernel,
        out_shape=(jax.ShapeDtypeStruct((PACK, COLS), BF), slots, slots, slots),
        in_specs=[vmem] * 4 + [hbm] * 4,
        out_specs=(vmem,) * 4,
        scratch_shapes=[
            pltpu.VMEM((3, SLOTS, COLS), BF),
            pltpu.VMEM((PACK, COLS), BF),
            pltpu.VMEM((6, NY, SLOTS // NY, COLS), BF),
            pltpu.VMEM((6, NY, SLOTS // NY, COLS), BF),
            pltpu.VMEM((6, NZ, SLOTS // NZ, COLS), BF),
            pltpu.VMEM((6, NZ, SLOTS // NZ, COLS), BF),
            pltpu.VMEM((3, 8, LANES), F32),
            pltpu.VMEM((3, TENSOR, 8, LANES), F32),
            square,
            square,
            pltpu.VMEM((PACK, SLOTS), BF),
            pltpu.VMEM((PACK, SLOTS), BF),
            pltpu.VMEM((SLOTS, PACK), BF),
            square,
            square,
            pltpu.VMEM((HEADS, PACK, PACK), F32),
            pltpu.VMEM((HEADS, PACK, PACK), F32),
            pltpu.VMEM((PACK, COLS), F32),
            pltpu.VMEM((PACK, COLS), F32),
            pltpu.VMEM((PACK, COLS), BF),
            pltpu.VMEM((PACK, COLS), BF),
            pltpu.VMEM((PACK, COLS), F32),
            pltpu.VMEM((PACK, COLS), F32),
            dma((4,)),
            dma((6,)),
            dma((6,)),
            dma((6,)),
            dma((6,)),
            dma((3,)),
            dma((3,)),
        ],
        compiler_params=pltpu.CompilerParams(
            collective_id=0, has_side_effects=True, vmem_limit_bytes=48 * 2**20
        ),
        cost_estimate=pl.CostEstimate(
            flops=4 * 10**9, bytes_accessed=3 * 10**6, transcendentals=10**6
        ),
        name="repack_attention",
    )(
        kept_mask.reshape(1, SLOTS),
        block_dest.reshape(1, SHARDS),
        pack_offset.reshape(1, SHARDS),
        pack_image.reshape(1, PACK),
        query_rows,
        key_rows,
        value_rows,
        grad_attended,
    )


def solution(mesh):
    in_specs = (
        P("dp", "tensor"),
        P("dp", "tensor"),
        P("dp", "tensor"),
        P("dp"),
        P("dp"),
        P("dp"),
        P("dp"),
        P("dp", "tensor"),
    )
    out_specs = (P("dp", "tensor"), P("dp", "tensor"), P("dp", "tensor"), P("dp", "tensor"))
    return jax.shard_map(local, mesh=mesh, in_specs=in_specs, out_specs=out_specs, check_vma=False)
```

time: 277 us -> 116 us (0.42)
  waiting for transfers between devices: 126 us -> 0 us
  Pallas kernels: 0 us -> 105 us
  starting transfers between devices: 58.8 us -> 0 us
  local copies, waits for them, and re-layouts: 41.1 us -> 8.69 us
  blocking collectives: 29.4 us -> 0 us
  matrix products: 12.2 us -> 0 us
  other arithmetic: 5.06 us -> 0 us
    all_to_all x6 -> x0, waiting for transfers between devices: 126 us -> none  [the longest x1 24.1 us: local(): lax.all_to_all(outgoing(query_rows), 'dp', split_axis=0, concat_axis=0, t...]
    pallas_call x0 -> x1, Pallas kernels: none -> 105 us  [local(): pl.pallas_call(kernel, out_shape=(jax.ShapeDtypeStruct((PACK, COLS), BF),...]
    all_to_all x6 -> x0, starting transfers between devices: 58.8 us -> none  [the longest x1 19.4 us: local(): lax.all_to_all(outgoing(query_rows), 'dp', split_axis=0, concat_axis=0, t...]
    psum x2 -> x0, blocking collectives: 29.4 us -> none  [the longest x1 17 us: local(): lax.psum((jnp.sum(query_float * query_float, axis=1), jnp.sum(key_float *...]
    gather x15 -> x0, local copies, waits for them, and re-layouts: 26.6 us -> none  [the longest x3 6.4 us: outgoing(): picked = jnp.take(source, send_rows, axis=0)]
    dot_general x6 -> x0, matrix products: 12.2 us -> none  [the longest x1 3.78 us: local(): jnp.einsum('hqk,khd->qhd', round_grad, round_key, preferred_element_type=...]
    unnamed x38 -> x20, local copies, waits for them, and re-layouts: 1.17 us -> 8.68 us
    reshape x16 -> x2, local copies, waits for them, and re-layouts: 7.1 us -> 0.01 us  [the longest x1 0.01 us: local(): kept_mask.reshape(1, SLOTS)]
  transfers between devices with their start and end apart: 6 -> 0, of which waited for: 6 -> 0; matrix products, arithmetic and copies ran while one was open for 7% -> 0% of each run, Pallas kernels for 0% -> 0%
where the time goes in v1:
time: 116 us; the launch traced here: 115 us
  Pallas kernels  105 us (91%)
  local copies, waits for them, and re-layouts  8.69 us (7%)
    pallas_call x1, Pallas kernels, local(): pl.pallas_call(kernel, out_shape=(jax.ShapeDtypeStruct((PACK, COLS), BF),...  105 us
    unnamed x20, local copies, waits for them, and re-layouts  8.68 us

profile of v1, /device:TPU:1, one launch (start us, length us, event | category | flops | bytes accessed | tf_op | source)
XLA Modules:
  0.0 114.7 jit_solution(16284485449451000177)
XLA Ops:
  0.6 0.0 copy-start.6
  0.6 0.7 copy-done.6
  1.3 0.0 copy-start.7
  1.3 0.7 copy-done.7
  2.0 0.0 copy-start.4
  2.0 0.0 copy-start.5
  2.0 0.6 copy-done.4
  2.7 0.0 copy-done.5
  2.7 0.0 copy-start
  2.7 1.0 copy-done
  3.6 0.0 copy-start.1
  3.6 1.0 copy-done.1
  4.6 0.0 copy-start.2
  4.6 1.0 copy-done.2
  5.6 0.0 copy-start.3
  5.6 0.9 copy-done.3
  6.5 105.4 %repack_attention.1 = (bf16[320,384]{1,0:T(8,128)(2,1)S(1)}, bf16[384,384]{1,0:T(8,128)(2,1)S(1)}, bf16[384,384]{1,0:T(8,128)(2,1)S(1)}, bf16[384,384]{1,0:T(8,128)(2,1)S(1)}) custom-call(s32[1,384]{1,0:T(1,128)S(1)} %reshape.20.kept_ref, s32[1,64]{1,0:T(1,128)S(1)} %bitcast.2, s32[1,64]{1,0:T(1,128)S(1)} %bitcast.3, s32[1,320]{1,0:T(1,128)S(1)} %reshape.23.image_ref, ...), custom_call_target="tpu_custom_call" | custom-call | flops 4000000000 | bytes 3000000 | tf_op jit(solution)/shard_map/repack_attention/pallas_call | solution.py:324
  111.9 0.7 copy.16
  112.6 0.7 copy.17
  113.3 0.7 copy.18
  114.0 0.7 copy.19
  (2 shorter events, 0.0 us)
Async XLA Ops:
  0.6 0.7 copy-start.6
  1.3 0.7 copy-start.7
  2.0 0.7 copy-start.4
  2.0 0.7 copy-start.5
  2.7 1.0 copy-start
  3.6 1.0 copy-start.1
  4.6 1.0 copy-start.2
  5.6 0.9 copy-start.3

commit v2 on v1

--- a/solution.py
+++ b/solution.py
@@ -25,6 +25,7 @@
 PACK = 320
 COLS = 384
 HEADS = COLS // HDIM
+FIRST = 8
 LANES = 384
 TENSOR = 8
 
@@ -67,12 +68,12 @@
 
 
 def kernel(
-    kept_ref, dest_ref, offset_ref, image_ref, q_hbm, k_hbm, v_hbm, g_hbm,
-    att_ref, dq_ref, dk_ref, dv_ref,
-    qkv, cot, ysend, yrecv, zsend, zrecv, xsend, xrecv,
-    gather_y, unpack, place, place_y, back_y, regroup, regroup_inv,
+    kept_hbm, dest_hbm, offset_hbm, image_hbm, q_hbm, k_hbm, v_hbm, g_hbm,
+    att_hbm, dq_hbm, dk_hbm, dv_hbm,
+    kept_ref, dest_ref, offset_ref, image_ref, qkv, cot, attended, home, ysend, yrecv, zsend, zrecv, xsend, xrecv,
+    gather_y, unpack, unpack_y, place, place_y, back, back_y, regroup, regroup_inv,
     probs, tanhs, packed_q, packed_k, normed_q, normed_k, grad_q, grad_k,
-    load_sem, ysend_sem, yrecv_sem, zsend_sem, zrecv_sem, xsend_sem, xrecv_sem,
+    load_sem, store_sem, ysend_sem, yrecv_sem, zsend_sem, zrecv_sem, xsend_sem, xrecv_sem,
 ):
     dp = lax.axis_index("dp")
     tensor = lax.axis_index("tensor")
@@ -82,7 +83,7 @@
         return lax.rem(y + i + 1, NY)
 
     def z_peer(i):
-        half = (i + 1) // 2 + (i + 1) % 2
+        half = NZ // 2 - (i + 1) // 2
         return lax.rem(z + jnp.where(i % 2 == 0, half, NZ - half), NZ)
 
     def x_peer(i):
@@ -113,11 +114,21 @@
     loads = [
         pltpu.make_async_copy(source, target, load_sem.at[i])
         for i, (source, target) in enumerate(
-            ((q_hbm, qkv.at[0]), (k_hbm, qkv.at[1]), (v_hbm, qkv.at[2]), (g_hbm, cot))
+            (
+                (kept_hbm, kept_ref), (dest_hbm, dest_ref), (offset_hbm, offset_ref),
+                (image_hbm, image_ref), (q_hbm, qkv.at[0]), (k_hbm, qkv.at[1]),
+                (v_hbm, qkv.at[2]), (g_hbm, cot),
+            )
         )
     ]
     for load in loads:
         load.start()
+    stores = [
+        pltpu.make_async_copy(source, target, store_sem.at[i])
+        for i, (source, target) in enumerate(
+            ((attended, att_hbm), (home.at[0], dv_hbm), (home.at[1], dq_hbm), (home.at[2], dk_hbm))
+        )
+    ]
 
     def send_y(array):
         def one(i, carry):
@@ -140,13 +151,19 @@
         def one(i, carry):
             peer = z_peer(i)
             pltpu.make_async_remote_copy(
-                zsend.at[array, peer], zrecv.at[array, z], zsend_sem.at[array], zrecv_sem.at[array],
+                zsend.at[array, peer], zrecv.at[array, z],
+                zsend_sem.at[array, jnp.where(i < FIRST, 0, 1)], zrecv_sem.at[array],
                 device_id={"dp": peer * NY + y}, device_id_type=MESH,
             ).start()
             return carry
 
         lax.fori_loop(0, NZ - 1, one, 0)
         zrecv[array, z] = zsend[array, z]
+
+    def wait_sent_z(array, half):
+        count = FIRST if half == 0 else NZ - 1 - FIRST
+        part = zsend.at[array, pl.ds(0, count)]
+        pltpu.make_async_copy(part, part, zsend_sem.at[array, half]).wait()
 
     def wait_z(array):
         part = zrecv.at[array, pl.ds(0, NZ - 1)]
@@ -183,12 +200,14 @@
     down = iota((SLOTS, SLOTS), 0)
     across = iota((SLOTS, SLOTS), 1)
     earlier = jnp.where((sixth(down) == sixth(across)) & (down < across), 1.0, 0.0).astype(BF)
-    kept = kept_ref[...]
+    for load in loads[:4]:
+        load.wait()
+    kept = kept_ref[...].reshape(1, SLOTS)
     before = mm(jnp.broadcast_to(kept.astype(F32), (8, SLOTS)).astype(BF), earlier)[0:1]
     before = before.astype(I32)
     which = iota((8, SHARDS), 0)
-    dest = dest_ref[...]
-    offset = offset_ref[...]
+    dest = dest_ref[...].reshape(1, SHARDS)
+    offset = offset_ref[...].reshape(1, SHARDS)
     parts = jnp.where(which == 0, dest, jnp.where(which == 1, offset >> 4, offset & 15))
     parts = parts.astype(F32).astype(BF)
     spread = mm(parts, one_hot(unit, SHARDS)).astype(I32)
@@ -201,38 +220,40 @@
     target_y = jnp.where(kept == 1, dest_y * BLOCK + before, -1)
 
     gather = one_hot(target, SLOTS)
-    loads[0].wait()
+    loads[4].wait()
     put_z(Q, mm(gather, qkv[0]))
     pl.semaphore_wait(barrier, (NZ - 1) + (NY - 1) + (TENSOR - 1))
     send_z(Q)
 
     gather_y[...] = one_hot(target_y, SLOTS)
-    loads[1].wait()
+    loads[5].wait()
     put_y(K, mm(gather_y[...], qkv[1]))
     send_y(K)
-    loads[2].wait()
+    loads[6].wait()
     put_y(V, mm(gather_y[...], qkv[2]))
     send_y(V)
 
     identity = jnp.where(down == across, 1.0, 0.0).astype(BF)
     regroup[...] = one_hot(unit_y * BLOCK + spot, SLOTS)
-    put_z(K, mm(regroup[...], wait_y(K)))
-    send_z(K)
-    put_z(V, mm(regroup[...], wait_y(V)))
-    send_z(V)
-
     unpack[...] = mm_nt(identity, gather).astype(BF)
     place[...] = one_hot(first + spot, PACK)
     place_y[...] = one_hot(first_y + spot, PACK)
+    back[...] = mm_nt(identity, place[...]).astype(BF)
     back_y[...] = mm_nt(identity, place_y[...]).astype(BF)
+    unpack_y[...] = mm_nt(identity, gather_y[...]).astype(BF)
     unit_n = (unit & (NY - 1)) * NZ + (unit >> 2)
     regroup_inv[...] = one_hot(unit_n * BLOCK + spot, SLOTS)
 
-    image = jnp.broadcast_to(image_ref[...], (8, PACK))
+    image = jnp.broadcast_to(image_ref[...].reshape(1, PACK), (8, PACK))
     image_hot = jnp.where(image == iota((8, PACK), 0), 1.0, 0.0).astype(BF)
     same = mm_tn(image_hot, image_hot)
 
     xsend[...] = jnp.zeros((3, 8, LANES), F32)
+
+    put_z(K, mm(regroup[...], wait_y(K)))
+    put_z(V, mm(regroup[...], wait_y(V)))
+    wait_sent_z(Q, 0)
+    send_z(K)
 
     put_y(Q, mm(regroup_inv[...], wait_z(Q)))
     send_y(Q)
@@ -240,6 +261,8 @@
     packed_q[...] = packed
     xsend[0, :, :PACK] = row_sums(packed * packed)
     send_x(0)
+    wait_sent_z(K, 0)
+    send_z(V)
 
     packed = mm(place[...], wait_z(K))
     packed_k[...] = packed
@@ -253,20 +276,19 @@
     packed_k[...] = packed_k[...] * scale_k
     normed_k[...] = packed_k[...].astype(BF)
 
-    loads[3].wait()
+    loads[7].wait()
     value_back = []
     for h in range(HEADS):
         cols = slice(h * HDIM, (h + 1) * HDIM)
         raw = mm_nt(normed_q[:, cols], normed_k[:, cols]) / math.sqrt(HDIM)
         bent = jnp.tanh(raw / SOFT_LIMIT)
         weight = jnp.exp(SOFT_LIMIT * bent) * same
-        prob = weight / jnp.sum(weight, axis=1, keepdims=True)
+        prob = weight * (1.0 / jnp.sum(weight, axis=1, keepdims=True))
         probs[h] = prob
         tanhs[h] = bent
         value_back.append(mm_tn(prob.astype(BF), cot[:, cols]).astype(BF))
-    put_y(DV, mm(back_y[...], jnp.concatenate(value_back, axis=1)))
-    send_y(DV)
-    put_z(DV, mm(regroup[...], wait_y(DV)))
+    put_z(DV, mm(back[...], jnp.concatenate(value_back, axis=1)))
+    wait_sent_z(V, 0)
     send_z(DV)
 
     value = mm(place[...], wait_z(V)).astype(BF)
@@ -286,49 +308,69 @@
     send_x(2)
     for h in range(HEADS):
         cols = slice(h * HDIM, (h + 1) * HDIM)
-        att_ref[:, cols] = mm(probs[h].astype(BF), value[:, cols]).astype(BF)
+        attended[:, cols] = mm(probs[h].astype(BF), value[:, cols]).astype(BF)
+    stores[0].start()
     inner = wait_x(2) / WIDTH
-    back = scale_q * (grad_q[...] - packed_q[...] * column(inner[0:1]))
-    put_y(DQ, mm(back_y[...], back.astype(BF)))
+    grad = scale_q * (grad_q[...] - packed_q[...] * column(inner[0:1]))
+    put_z(DQ, mm(back[...], grad.astype(BF)))
+    grad = scale_k * (grad_k[...] - packed_k[...] * column(inner[1:2]))
+    put_y(DK, mm(back_y[...], grad.astype(BF)))
+    wait_sent_z(DV, 0)
+    send_z(DQ)
+    send_y(DK)
+    put_z(DK, mm(regroup[...], wait_y(DK)))
+    put_y(DV, mm(regroup_inv[...], wait_z(DV)))
+    send_y(DV)
+    wait_sent_z(DQ, 0)
+    send_z(DK)
+    home[0] = mm(unpack_y[...], wait_y(DV)).astype(BF)
+    stores[1].start()
+    put_y(DQ, mm(regroup_inv[...], wait_z(DQ)))
     send_y(DQ)
-    back = scale_k * (grad_k[...] - packed_k[...] * column(inner[1:2]))
-    put_y(DK, mm(back_y[...], back.astype(BF)))
-    send_y(DK)
-    put_z(DQ, mm(regroup[...], wait_y(DQ)))
-    send_z(DQ)
-    put_z(DK, mm(regroup[...], wait_y(DK)))
-    send_z(DK)
-
-    dv_ref[...] = mm(unpack[...], wait_z(DV)).astype(BF)
-    dq_ref[...] = mm(unpack[...], wait_z(DQ)).astype(BF)
-    dk_ref[...] = mm(unpack[...], wait_z(DK)).astype(BF)
+    home[1] = mm(unpack_y[...], wait_y(DQ)).astype(BF)
+    stores[2].start()
+    home[2] = mm(unpack[...], wait_z(DK)).astype(BF)
+    stores[3].start()
 
     for array in range(6):
         part = ysend.at[array, pl.ds(0, NY - 1)]
         pltpu.make_async_copy(part, part, ysend_sem.at[array]).wait()
-        part = zsend.at[array, pl.ds(0, NZ - 1)]
-        pltpu.make_async_copy(part, part, zsend_sem.at[array]).wait()
+        wait_sent_z(array, 1)
+    wait_sent_z(DK, 0)
     for which in range(3):
         part = xrecv.at[which, pl.ds(0, TENSOR - 1)]
         pltpu.make_async_copy(part, part, xsend_sem.at[which]).wait()
+    for copy in stores:
+        copy.wait()
+
+
+def store(*refs):
+    for source, target in zip(refs[:4], refs[4:]):
+        target[...] = source[...]
 
 
 def local(
     query_rows, key_rows, value_rows, kept_mask, block_dest, pack_offset, pack_image, grad_attended
 ):
+    hbm = pl.BlockSpec(memory_space=pltpu.HBM)
     vmem = pl.BlockSpec(memory_space=pltpu.VMEM)
-    hbm = pl.BlockSpec(memory_space=pl.ANY)
     dma = pltpu.SemaphoreType.DMA
     slots = jax.ShapeDtypeStruct((SLOTS, COLS), BF)
     square = pltpu.VMEM((SLOTS, SLOTS), BF)
-    return pl.pallas_call(
+    results = pl.pallas_call(
         kernel,
         out_shape=(jax.ShapeDtypeStruct((PACK, COLS), BF), slots, slots, slots),
-        in_specs=[vmem] * 4 + [hbm] * 4,
-        out_specs=(vmem,) * 4,
+        in_specs=[hbm] * 8,
+        out_specs=(hbm,) * 4,
         scratch_shapes=[
+            pltpu.VMEM((SLOTS,), I32),
+            pltpu.VMEM((SHARDS,), I32),
+            pltpu.VMEM((SHARDS,), I32),
+            pltpu.VMEM((PACK,), I32),
             pltpu.VMEM((3, SLOTS, COLS), BF),
             pltpu.VMEM((PACK, COLS), BF),
+            pltpu.VMEM((PACK, COLS), BF),
+            pltpu.VMEM((3, SLOTS, COLS), BF),
             pltpu.VMEM((6, NY, SLOTS // NY, COLS), BF),
             pltpu.VMEM((6, NY, SLOTS // NY, COLS), BF),
             pltpu.VMEM((6, NZ, SLOTS // NZ, COLS), BF),
@@ -337,8 +379,10 @@
             pltpu.VMEM((3, TENSOR, 8, LANES), F32),
             square,
             square,
+            square,
             pltpu.VMEM((PACK, SLOTS), BF),
             pltpu.VMEM((PACK, SLOTS), BF),
+            pltpu.VMEM((SLOTS, PACK), BF),
             pltpu.VMEM((SLOTS, PACK), BF),
             square,
             square,
@@ -350,31 +394,40 @@
             pltpu.VMEM((PACK, COLS), BF),
             pltpu.VMEM((PACK, COLS), F32),
             pltpu.VMEM((PACK, COLS), F32),
+            dma((8,)),
             dma((4,)),
             dma((6,)),
             dma((6,)),
-            dma((6,)),
+            dma((6, 2)),
             dma((6,)),
             dma((3,)),
             dma((3,)),
         ],
         compiler_params=pltpu.CompilerParams(
-            collective_id=0, has_side_effects=True, vmem_limit_bytes=48 * 2**20
+            collective_id=0, has_side_effects=True, vmem_limit_bytes=62 * 2**20
         ),
         cost_estimate=pl.CostEstimate(
             flops=4 * 10**9, bytes_accessed=3 * 10**6, transcendentals=10**6
         ),
         name="repack_attention",
     )(
-        kept_mask.reshape(1, SLOTS),
-        block_dest.reshape(1, SHARDS),
-        pack_offset.reshape(1, SHARDS),
-        pack_image.reshape(1, PACK),
+        kept_mask,
+        block_dest,
+        pack_offset,
+        pack_image,
         query_rows,
         key_rows,
         value_rows,
         grad_attended,
     )
+    return pl.pallas_call(
+        store,
+        out_shape=(jax.ShapeDtypeStruct((PACK, COLS), BF), slots, slots, slots),
+        in_specs=[vmem] * 4,
+        out_specs=(vmem,) * 4,
+        compiler_params=pltpu.CompilerParams(vmem_limit_bytes=62 * 2**20),
+        name="store_outputs",
+    )(*results)
 
 
 def solution(mesh):

time: 116 us -> 98.2 us (0.85)
  local copies, waits for them, and re-layouts: 8.69 us -> 0 us
  Pallas kernels: 105 us -> 97.4 us
    pallas_call x1, Pallas kernels: 105 us -> 95.1 us  [local(): pl.pallas_call(kernel, out_shape=(jax.ShapeDtypeStruct((PACK, COLS), BF),...]
    unnamed x20 -> x0, local copies, waits for them, and re-layouts: 8.68 us -> none
    pallas_call x0 -> x1, Pallas kernels: none -> 2.28 us  [local(): pl.pallas_call(store, out_shape=(jax.ShapeDtypeStruct((PACK, COLS), BF),...]
where the time goes in v2:
time: 98.2 us; the launch traced here: 98 us
  Pallas kernels  97.4 us (99%)
    pallas_call x1, Pallas kernels, local(): pl.pallas_call(kernel, out_shape=(jax.ShapeDtypeStruct((PACK, COLS), BF),...  95.1 us
    pallas_call x1, Pallas kernels, local(): pl.pallas_call(store, out_shape=(jax.ShapeDtypeStruct((PACK, COLS), BF),...  2.28 us

profile of v2, /device:TPU:1, one launch (start us, length us, event | category | flops | bytes accessed | tf_op | source)
XLA Modules:
  0.0 98.0 jit_solution(11168229585593185735)
XLA Ops:
  0.6 95.1 %repack_attention.1 = (bf16[320,384]{1,0:T(8,128)(2,1)}, bf16[384,384]{1,0:T(8,128)(2,1)}, bf16[384,384]{1,0:T(8,128)(2,1)}, bf16[384,384]{1,0:T(8,128)(2,1)}) custom-call(s32[384]{0:T(512)} %kept_hbm.1, s32[64]{0:T(128)} %dest_hbm.1, s32[64]{0:T(128)} %offset_hbm.1, s32[320]{0:T(512)} %image_hbm.1, bf16[384,384]{1,0:T(8,128)(2,1)} %q_hbm.1, ...), custom_call_target="tpu_custom_call" | custom-call | flops 4000000000 | bytes 3000000 | tf_op jit(solution)/shard_map/repack_attention/pallas_call | solution.py:360
  95.8 2.3 %store_outputs.1 = (bf16[320,384]{1,0:T(8,128)(2,1)}, bf16[384,384]{1,0:T(8,128)(2,1)}, bf16[384,384]{1,0:T(8,128)(2,1)}, bf16[384,384]{1,0:T(8,128)(2,1)}) custom-call(bf16[320,384]{1,0:T(8,128)(2,1)} %get-tuple-element.8.refs_0_, bf16[384,384]{1,0:T(8,128)(2,1)} %get-tuple-element.9.refs_1_, bf16[384,384]{1,0:T(8,128)(2,1)} %get-tuple-element.10.refs_2_, ...), custom_call_target="tpu_custom_call" | custom-call | tf_op jit(solution)/shard_map/store_outputs/pallas_call | solution.py:423

commit v3 on v2

--- a/solution.py
+++ b/solution.py
@@ -25,7 +25,7 @@
 PACK = 320
 COLS = 384
 HEADS = COLS // HDIM
-FIRST = 8
+FAR = 7
 LANES = 384
 TENSOR = 8
 
@@ -73,7 +73,7 @@
     kept_ref, dest_ref, offset_ref, image_ref, qkv, cot, attended, home, ysend, yrecv, zsend, zrecv, xsend, xrecv,
     gather_y, unpack, unpack_y, place, place_y, back, back_y, regroup, regroup_inv,
     probs, tanhs, packed_q, packed_k, normed_q, normed_k, grad_q, grad_k,
-    load_sem, store_sem, ysend_sem, yrecv_sem, zsend_sem, zrecv_sem, xsend_sem, xrecv_sem,
+    far_sem, load_sem, store_sem, ysend_sem, yrecv_sem, zsend_sem, zrecv_sem, xsend_sem, xrecv_sem,
 ):
     dp = lax.axis_index("dp")
     tensor = lax.axis_index("tensor")
@@ -88,28 +88,6 @@
 
     def x_peer(i):
         return lax.rem(tensor + i + 1, TENSOR)
-
-    barrier = pltpu.get_barrier_semaphore()
-
-    def greet_z(i, carry):
-        pl.semaphore_signal(
-            barrier, inc=1, device_id={"dp": z_peer(i) * NY + y}, device_id_type=MESH
-        )
-        return carry
-
-    def greet_y(i, carry):
-        pl.semaphore_signal(
-            barrier, inc=1, device_id={"dp": z * NY + y_peer(i)}, device_id_type=MESH
-        )
-        return carry
-
-    def greet_x(i, carry):
-        pl.semaphore_signal(barrier, inc=1, device_id={"tensor": x_peer(i)}, device_id_type=MESH)
-        return carry
-
-    lax.fori_loop(0, NZ - 1, greet_z, 0)
-    lax.fori_loop(0, NY - 1, greet_y, 0)
-    lax.fori_loop(0, TENSOR - 1, greet_x, 0)
 
     loads = [
         pltpu.make_async_copy(source, target, load_sem.at[i])
@@ -123,6 +101,28 @@
     ]
     for load in loads:
         load.start()
+    barrier = pltpu.get_barrier_semaphore()
+
+    def greet_z(i, carry):
+        pl.semaphore_signal(
+            barrier, inc=1, device_id={"dp": z_peer(i) * NY + y}, device_id_type=MESH
+        )
+        return carry
+
+    def greet_y(i, carry):
+        pl.semaphore_signal(
+            barrier, inc=1, device_id={"dp": z * NY + y_peer(i)}, device_id_type=MESH
+        )
+        return carry
+
+    def greet_x(i, carry):
+        pl.semaphore_signal(barrier, inc=1, device_id={"tensor": x_peer(i)}, device_id_type=MESH)
+        return carry
+
+    lax.fori_loop(FAR, NZ - 1, greet_z, 0)
+    lax.fori_loop(0, NY - 1, greet_y, 0)
+    lax.fori_loop(0, TENSOR - 1, greet_x, 0)
+
     stores = [
         pltpu.make_async_copy(source, target, store_sem.at[i])
         for i, (source, target) in enumerate(
@@ -147,23 +147,18 @@
         pltpu.make_async_copy(part, part, yrecv_sem.at[array]).wait()
         return yrecv[array].reshape(SLOTS, COLS)
 
-    def send_z(array):
+    def send_z(array, first=0, last=NZ - 1):
         def one(i, carry):
             peer = z_peer(i)
             pltpu.make_async_remote_copy(
-                zsend.at[array, peer], zrecv.at[array, z],
-                zsend_sem.at[array, jnp.where(i < FIRST, 0, 1)], zrecv_sem.at[array],
+                zsend.at[array, peer], zrecv.at[array, z], zsend_sem.at[array], zrecv_sem.at[array],
                 device_id={"dp": peer * NY + y}, device_id_type=MESH,
             ).start()
             return carry
 
-        lax.fori_loop(0, NZ - 1, one, 0)
-        zrecv[array, z] = zsend[array, z]
-
-    def wait_sent_z(array, half):
-        count = FIRST if half == 0 else NZ - 1 - FIRST
-        part = zsend.at[array, pl.ds(0, count)]
-        pltpu.make_async_copy(part, part, zsend_sem.at[array, half]).wait()
+        lax.fori_loop(first, last, one, 0)
+        if first == 0:
+            zrecv[array, z] = zsend[array, z]
 
     def wait_z(array):
         part = zrecv.at[array, pl.ds(0, NZ - 1)]
@@ -222,8 +217,16 @@
     gather = one_hot(target, SLOTS)
     loads[4].wait()
     put_z(Q, mm(gather, qkv[0]))
-    pl.semaphore_wait(barrier, (NZ - 1) + (NY - 1) + (TENSOR - 1))
-    send_z(Q)
+    pl.semaphore_wait(barrier, (NZ - 1 - FAR) + (NY - 1) + (TENSOR - 1))
+
+    def pass_on(i, carry):
+        pl.semaphore_signal(
+            far_sem, inc=1, device_id={"dp": z_peer(i) * NY + y}, device_id_type=MESH
+        )
+        return carry
+
+    lax.fori_loop(FAR, FAR + 2, pass_on, 0)
+    send_z(Q, FAR, NZ - 1)
 
     gather_y[...] = one_hot(target_y, SLOTS)
     loads[5].wait()
@@ -232,6 +235,9 @@
     loads[6].wait()
     put_y(V, mm(gather_y[...], qkv[2]))
     send_y(V)
+
+    pl.semaphore_wait(far_sem, 2)
+    send_z(Q, 0, FAR)
 
     identity = jnp.where(down == across, 1.0, 0.0).astype(BF)
     regroup[...] = one_hot(unit_y * BLOCK + spot, SLOTS)
@@ -252,7 +258,6 @@
 
     put_z(K, mm(regroup[...], wait_y(K)))
     put_z(V, mm(regroup[...], wait_y(V)))
-    wait_sent_z(Q, 0)
     send_z(K)
 
     put_y(Q, mm(regroup_inv[...], wait_z(Q)))
@@ -261,7 +266,6 @@
     packed_q[...] = packed
     xsend[0, :, :PACK] = row_sums(packed * packed)
     send_x(0)
-    wait_sent_z(K, 0)
     send_z(V)
 
     packed = mm(place[...], wait_z(K))
@@ -288,7 +292,6 @@
         tanhs[h] = bent
         value_back.append(mm_tn(prob.astype(BF), cot[:, cols]).astype(BF))
     put_z(DV, mm(back[...], jnp.concatenate(value_back, axis=1)))
-    wait_sent_z(V, 0)
     send_z(DV)
 
     value = mm(place[...], wait_z(V)).astype(BF)
@@ -315,13 +318,11 @@
     put_z(DQ, mm(back[...], grad.astype(BF)))
     grad = scale_k * (grad_k[...] - packed_k[...] * column(inner[1:2]))
     put_y(DK, mm(back_y[...], grad.astype(BF)))
-    wait_sent_z(DV, 0)
     send_z(DQ)
     send_y(DK)
     put_z(DK, mm(regroup[...], wait_y(DK)))
     put_y(DV, mm(regroup_inv[...], wait_z(DV)))
     send_y(DV)
-    wait_sent_z(DQ, 0)
     send_z(DK)
     home[0] = mm(unpack_y[...], wait_y(DV)).astype(BF)
     stores[1].start()
@@ -335,8 +336,8 @@
     for array in range(6):
         part = ysend.at[array, pl.ds(0, NY - 1)]
         pltpu.make_async_copy(part, part, ysend_sem.at[array]).wait()
-        wait_sent_z(array, 1)
-    wait_sent_z(DK, 0)
+        part = zsend.at[array, pl.ds(0, NZ - 1)]
+        pltpu.make_async_copy(part, part, zsend_sem.at[array]).wait()
     for which in range(3):
         part = xrecv.at[which, pl.ds(0, TENSOR - 1)]
         pltpu.make_async_copy(part, part, xsend_sem.at[which]).wait()
@@ -394,11 +395,12 @@
             pltpu.VMEM((PACK, COLS), BF),
             pltpu.VMEM((PACK, COLS), F32),
             pltpu.VMEM((PACK, COLS), F32),
+            pltpu.SemaphoreType.REGULAR,
             dma((8,)),
             dma((4,)),
             dma((6,)),
             dma((6,)),
-            dma((6, 2)),
+            dma((6,)),
             dma((6,)),
             dma((3,)),
             dma((3,)),

time: 98.2 us -> 96.6 us (0.984)
  Pallas kernels: 97.4 us -> 95.8 us
    pallas_call x1, Pallas kernels: 95.1 us -> 93.5 us  [local(): pl.pallas_call(kernel, out_shape=(jax.ShapeDtypeStruct((PACK, COLS), BF),...]
where the time goes in v3:
time: 96.6 us; the launch traced here: 96.4 us
  Pallas kernels  95.8 us (99%)
    pallas_call x1, Pallas kernels, local(): pl.pallas_call(kernel, out_shape=(jax.ShapeDtypeStruct((PACK, COLS), BF),...  93.5 us
    pallas_call x1, Pallas kernels, local(): pl.pallas_call(store, out_shape=(jax.ShapeDtypeStruct((PACK, COLS), BF),...  2.28 us

profile of v3, /device:TPU:1, one launch (start us, length us, event | category | flops | bytes accessed | tf_op | source)
XLA Modules:
  0.0 96.4 jit_solution(2598357207837624206)
XLA Ops:
  0.6 93.5 %repack_attention.1 = (bf16[320,384]{1,0:T(8,128)(2,1)}, bf16[384,384]{1,0:T(8,128)(2,1)}, bf16[384,384]{1,0:T(8,128)(2,1)}, bf16[384,384]{1,0:T(8,128)(2,1)}) custom-call(s32[384]{0:T(512)} %kept_hbm.1, s32[64]{0:T(128)} %dest_hbm.1, s32[64]{0:T(128)} %offset_hbm.1, s32[320]{0:T(512)} %image_hbm.1, bf16[384,384]{1,0:T(8,128)(2,1)} %q_hbm.1, ...), custom_call_target="tpu_custom_call" | custom-call | flops 4000000000 | bytes 3000000 | tf_op jit(solution)/shard_map/repack_attention/pallas_call | solution.py:361
  94.1 2.3 %store_outputs.1 = (bf16[320,384]{1,0:T(8,128)(2,1)}, bf16[384,384]{1,0:T(8,128)(2,1)}, bf16[384,384]{1,0:T(8,128)(2,1)}, bf16[384,384]{1,0:T(8,128)(2,1)}) custom-call(bf16[320,384]{1,0:T(8,128)(2,1)} %get-tuple-element.8.refs_0_, bf16[384,384]{1,0:T(8,128)(2,1)} %get-tuple-element.9.refs_1_, bf16[384,384]{1,0:T(8,128)(2,1)} %get-tuple-element.10.refs_2_, ...), custom_call_target="tpu_custom_call" | custom-call | tf_op jit(solution)/shard_map/store_outputs/pallas_call | solution.py:425

commit v4 on v3

--- a/solution.py
+++ b/solution.py
@@ -69,11 +69,11 @@
 
 def kernel(
     kept_hbm, dest_hbm, offset_hbm, image_hbm, q_hbm, k_hbm, v_hbm, g_hbm,
-    att_hbm, dq_hbm, dk_hbm, dv_hbm,
+    att_hbm, dq_hbm, dv_hbm, last_hbm, unpack_hbm,
     kept_ref, dest_ref, offset_ref, image_ref, qkv, cot, attended, home, ysend, yrecv, zsend, zrecv, xsend, xrecv,
     gather_y, unpack, unpack_y, place, place_y, back, back_y, regroup, regroup_inv,
-    probs, tanhs, packed_q, packed_k, normed_q, normed_k, grad_q, grad_k,
-    far_sem, load_sem, store_sem, ysend_sem, yrecv_sem, zsend_sem, zrecv_sem, xsend_sem, xrecv_sem,
+    probs, tanhs, scores, packed_q, packed_k, normed_q, normed_k, grad_q, grad_k,
+    far_sem, own_sem, load_sem, store_sem, ysend_sem, yrecv_sem, zsend_sem, zrecv_sem, xsend_sem, xrecv_sem,
 ):
     dp = lax.axis_index("dp")
     tensor = lax.axis_index("tensor")
@@ -123,10 +123,11 @@
     lax.fori_loop(0, NY - 1, greet_y, 0)
     lax.fori_loop(0, TENSOR - 1, greet_x, 0)
 
+    own_last = pltpu.make_async_copy(zsend.at[DK, z], last_hbm.at[z], own_sem)
     stores = [
         pltpu.make_async_copy(source, target, store_sem.at[i])
         for i, (source, target) in enumerate(
-            ((attended, att_hbm), (home.at[0], dv_hbm), (home.at[1], dq_hbm), (home.at[2], dk_hbm))
+            ((attended, att_hbm), (home.at[0], dv_hbm), (home.at[1], dq_hbm), (unpack, unpack_hbm))
         )
     ]
 
@@ -148,16 +149,20 @@
         return yrecv[array].reshape(SLOTS, COLS)
 
     def send_z(array, first=0, last=NZ - 1):
+        target = last_hbm if array == DK else zrecv.at[array]
+
         def one(i, carry):
             peer = z_peer(i)
             pltpu.make_async_remote_copy(
-                zsend.at[array, peer], zrecv.at[array, z], zsend_sem.at[array], zrecv_sem.at[array],
+                zsend.at[array, peer], target.at[z], zsend_sem.at[array], zrecv_sem.at[array],
                 device_id={"dp": peer * NY + y}, device_id_type=MESH,
             ).start()
             return carry
 
         lax.fori_loop(first, last, one, 0)
-        if first == 0:
+        if array == DK:
+            own_last.start()
+        elif first == 0:
             zrecv[array, z] = zsend[array, z]
 
     def wait_z(array):
@@ -206,13 +211,8 @@
     parts = jnp.where(which == 0, dest, jnp.where(which == 1, offset >> 4, offset & 15))
     parts = parts.astype(F32).astype(BF)
     spread = mm(parts, one_hot(unit, SHARDS)).astype(I32)
-    spread_y = mm(parts, one_hot(unit_y, SHARDS)).astype(I32)
     dest_slot = spread[0:1]
-    first = spread[1:2] * 16 + spread[2:3]
-    first_y = spread_y[1:2] * 16 + spread_y[2:3]
-    dest_y = (dest_slot & (NY - 1)) * NZ + (dest_slot >> 2)
     target = jnp.where(kept == 1, dest_slot * BLOCK + before, -1)
-    target_y = jnp.where(kept == 1, dest_y * BLOCK + before, -1)
 
     gather = one_hot(target, SLOTS)
     loads[4].wait()
@@ -228,7 +228,8 @@
     lax.fori_loop(FAR, FAR + 2, pass_on, 0)
     send_z(Q, FAR, NZ - 1)
 
-    gather_y[...] = one_hot(target_y, SLOTS)
+    dest_y = (dest_slot & (NY - 1)) * NZ + (dest_slot >> 2)
+    gather_y[...] = one_hot(jnp.where(kept == 1, dest_y * BLOCK + before, -1), SLOTS)
     loads[5].wait()
     put_y(K, mm(gather_y[...], qkv[1]))
     send_y(K)
@@ -242,6 +243,10 @@
     identity = jnp.where(down == across, 1.0, 0.0).astype(BF)
     regroup[...] = one_hot(unit_y * BLOCK + spot, SLOTS)
     unpack[...] = mm_nt(identity, gather).astype(BF)
+    stores[3].start()
+    spread_y = mm(parts, one_hot(unit_y, SHARDS)).astype(I32)
+    first = spread[1:2] * 16 + spread[2:3]
+    first_y = spread_y[1:2] * 16 + spread_y[2:3]
     place[...] = one_hot(first + spot, PACK)
     place_y[...] = one_hot(first_y + spot, PACK)
     back[...] = mm_nt(identity, place[...]).astype(BF)
@@ -254,7 +259,7 @@
     image_hot = jnp.where(image == iota((8, PACK), 0), 1.0, 0.0).astype(BF)
     same = mm_tn(image_hot, image_hot)
 
-    xsend[...] = jnp.zeros((3, 8, LANES), F32)
+    xsend[...] = jnp.zeros((4, 8, LANES), F32)
 
     put_z(K, mm(regroup[...], wait_y(K)))
     put_z(V, mm(regroup[...], wait_y(V)))
@@ -302,23 +307,26 @@
         prob_grad = mm_nt(cot[:, cols], value[:, cols])
         inner = jnp.sum(prob * prob_grad, axis=1, keepdims=True)
         score = prob * (prob_grad - inner) * (1.0 - bent * bent) / math.sqrt(HDIM)
-        score = score.astype(BF)
-        grad_q[:, cols] = mm(score, normed_k[:, cols])
-        grad_k[:, cols] = mm_tn(score, normed_q[:, cols])
-    sums_q = row_sums(grad_q[...] * packed_q[...])
-    sums_k = row_sums(grad_k[...] * packed_k[...])
-    xsend[2, :, :PACK] = jnp.where(iota((8, PACK), 0) == 0, sums_q, sums_k)
+        scores[h] = score.astype(BF)
+        grad_q[:, cols] = mm(scores[h], normed_k[:, cols])
+    xsend[2, :, :PACK] = row_sums(grad_q[...] * packed_q[...])
     send_x(2)
+    for h in range(HEADS):
+        cols = slice(h * HDIM, (h + 1) * HDIM)
+        grad_k[:, cols] = mm_tn(scores[h], normed_q[:, cols])
+    xsend[3, :, :PACK] = row_sums(grad_k[...] * packed_k[...])
+    send_x(3)
     for h in range(HEADS):
         cols = slice(h * HDIM, (h + 1) * HDIM)
         attended[:, cols] = mm(probs[h].astype(BF), value[:, cols]).astype(BF)
     stores[0].start()
-    inner = wait_x(2) / WIDTH
-    grad = scale_q * (grad_q[...] - packed_q[...] * column(inner[0:1]))
+    inner = column(wait_x(2)[0:1] / WIDTH)
+    grad = scale_q * (grad_q[...] - packed_q[...] * inner)
     put_z(DQ, mm(back[...], grad.astype(BF)))
-    grad = scale_k * (grad_k[...] - packed_k[...] * column(inner[1:2]))
+    send_z(DQ)
+    inner = column(wait_x(3)[0:1] / WIDTH)
+    grad = scale_k * (grad_k[...] - packed_k[...] * inner)
     put_y(DK, mm(back_y[...], grad.astype(BF)))
-    send_z(DQ)
     send_y(DK)
     put_z(DK, mm(regroup[...], wait_y(DK)))
     put_y(DV, mm(regroup_inv[...], wait_z(DV)))
@@ -330,39 +338,69 @@
     send_y(DQ)
     home[1] = mm(unpack_y[...], wait_y(DQ)).astype(BF)
     stores[2].start()
-    home[2] = mm(unpack[...], wait_z(DK)).astype(BF)
-    stores[3].start()
+    part = last_hbm.at[pl.ds(0, NZ - 1)]
+    pltpu.make_async_copy(part, part, zrecv_sem.at[DK]).wait()
+    own_last.wait()
 
     for array in range(6):
         part = ysend.at[array, pl.ds(0, NY - 1)]
         pltpu.make_async_copy(part, part, ysend_sem.at[array]).wait()
         part = zsend.at[array, pl.ds(0, NZ - 1)]
         pltpu.make_async_copy(part, part, zsend_sem.at[array]).wait()
-    for which in range(3):
+    for which in range(4):
         part = xrecv.at[which, pl.ds(0, TENSOR - 1)]
         pltpu.make_async_copy(part, part, xsend_sem.at[which]).wait()
     for copy in stores:
         copy.wait()
 
 
-def store(*refs):
-    for source, target in zip(refs[:4], refs[4:]):
-        target[...] = source[...]
+def finish(
+    att_in, dq_in, dv_in, last_in, unpack_in, att_out, dq_out, dk_out, dv_out,
+    att, dq, dv, last, unpack, dk, load_sem, store_sem,
+):
+    loads = [
+        pltpu.make_async_copy(source, target, load_sem.at[i])
+        for i, (source, target) in enumerate(
+            ((last_in, last), (unpack_in, unpack), (att_in, att), (dq_in, dq), (dv_in, dv))
+        )
+    ]
+    stores = [
+        pltpu.make_async_copy(source, target, store_sem.at[i])
+        for i, (source, target) in enumerate(
+            ((att, att_out), (dq, dq_out), (dv, dv_out), (dk, dk_out))
+        )
+    ]
+    for load in loads:
+        load.start()
+    loads[0].wait()
+    loads[1].wait()
+    dk[...] = mm(unpack[...], last[...].reshape(SLOTS, COLS)).astype(BF)
+    stores[3].start()
+    for i in range(3):
+        loads[i + 2].wait()
+        stores[i].start()
+    for copy in stores:
+        copy.wait()
 
 
 def local(
     query_rows, key_rows, value_rows, kept_mask, block_dest, pack_offset, pack_image, grad_attended
 ):
     hbm = pl.BlockSpec(memory_space=pltpu.HBM)
-    vmem = pl.BlockSpec(memory_space=pltpu.VMEM)
     dma = pltpu.SemaphoreType.DMA
     slots = jax.ShapeDtypeStruct((SLOTS, COLS), BF)
     square = pltpu.VMEM((SLOTS, SLOTS), BF)
     results = pl.pallas_call(
         kernel,
-        out_shape=(jax.ShapeDtypeStruct((PACK, COLS), BF), slots, slots, slots),
+        out_shape=(
+            jax.ShapeDtypeStruct((PACK, COLS), BF),
+            slots,
+            slots,
+            jax.ShapeDtypeStruct((NZ, SLOTS // NZ, COLS), BF),
+            jax.ShapeDtypeStruct((SLOTS, SLOTS), BF),
+        ),
         in_specs=[hbm] * 8,
-        out_specs=(hbm,) * 4,
+        out_specs=(hbm,) * 5,
         scratch_shapes=[
             pltpu.VMEM((SLOTS,), I32),
             pltpu.VMEM((SHARDS,), I32),
@@ -376,8 +414,8 @@
             pltpu.VMEM((6, NY, SLOTS // NY, COLS), BF),
             pltpu.VMEM((6, NZ, SLOTS // NZ, COLS), BF),
             pltpu.VMEM((6, NZ, SLOTS // NZ, COLS), BF),
-            pltpu.VMEM((3, 8, LANES), F32),
-            pltpu.VMEM((3, TENSOR, 8, LANES), F32),
+            pltpu.VMEM((4, 8, LANES), F32),
+            pltpu.VMEM((4, TENSOR, 8, LANES), F32),
             square,
             square,
             square,
@@ -389,6 +427,7 @@
             square,
             pltpu.VMEM((HEADS, PACK, PACK), F32),
             pltpu.VMEM((HEADS, PACK, PACK), F32),
+            pltpu.VMEM((HEADS, PACK, PACK), BF),
             pltpu.VMEM((PACK, COLS), F32),
             pltpu.VMEM((PACK, COLS), F32),
             pltpu.VMEM((PACK, COLS), BF),
@@ -396,14 +435,15 @@
             pltpu.VMEM((PACK, COLS), F32),
             pltpu.VMEM((PACK, COLS), F32),
             pltpu.SemaphoreType.REGULAR,
+            dma,
             dma((8,)),
             dma((4,)),
             dma((6,)),
             dma((6,)),
             dma((6,)),
             dma((6,)),
-            dma((3,)),
-            dma((3,)),
+            dma((4,)),
+            dma((4,)),
         ],
         compiler_params=pltpu.CompilerParams(
             collective_id=0, has_side_effects=True, vmem_limit_bytes=62 * 2**20
@@ -423,12 +463,22 @@
         grad_attended,
     )
     return pl.pallas_call(
-        store,
+        finish,
         out_shape=(jax.ShapeDtypeStruct((PACK, COLS), BF), slots, slots, slots),
-        in_specs=[vmem] * 4,
-        out_specs=(vmem,) * 4,
+        in_specs=[hbm] * 5,
+        out_specs=(hbm,) * 4,
+        scratch_shapes=[
+            pltpu.VMEM((PACK, COLS), BF),
+            pltpu.VMEM((SLOTS, COLS), BF),
+            pltpu.VMEM((SLOTS, COLS), BF),
+            pltpu.VMEM((NZ, SLOTS // NZ, COLS), BF),
+            pltpu.VMEM((SLOTS, SLOTS), BF),
+            pltpu.VMEM((SLOTS, COLS), BF),
+            dma((5,)),
+            dma((4,)),
+        ],
         compiler_params=pltpu.CompilerParams(vmem_limit_bytes=62 * 2**20),
-        name="store_outputs",
+        name="finish",
     )(*results)
 
 

time: 96.6 us -> 95.5 us (0.989)
  Pallas kernels: 95.8 us -> 94.7 us
    pallas_call x1, Pallas kernels: 93.5 us -> 92.2 us  [local(): pl.pallas_call(kernel, out_shape=(jax.ShapeDtypeStruct((PACK, COLS), BF),...]
where the time goes in v4:
time: 95.5 us; the launch traced here: 95.3 us
  Pallas kernels  94.7 us (99%)
    pallas_call x1, Pallas kernels, local(): pl.pallas_call(kernel, out_shape=(jax.ShapeDtypeStruct((PACK, COLS), BF),...  92.2 us
    pallas_call x1, Pallas kernels, local(): pl.pallas_call(finish, out_shape=(jax.ShapeDtypeStruct((PACK, COLS), BF),...  2.45 us

profile of v4, /device:TPU:1, one launch (start us, length us, event | category | flops | bytes accessed | tf_op | source)
XLA Modules:
  0.0 95.3 jit_solution(16215468694218196270)
XLA Ops:
  0.6 92.2 %repack_attention.1 = (bf16[320,384]{1,0:T(8,128)(2,1)}, bf16[384,384]{1,0:T(8,128)(2,1)}, bf16[384,384]{1,0:T(8,128)(2,1)}, bf16[16,24,384]{2,1,0:T(8,128)(2,1)}, bf16[384,384]{1,0:T(8,128)(2,1)}) custom-call(s32[384]{0:T(512)} %kept_hbm.1, s32[64]{0:T(128)} %dest_hbm.1, s32[64]{0:T(128)} %offset_hbm.1, s32[320]{0:T(512)} %image_hbm.1, ...), custom_call_target="tpu_custom_call" | custom-call | flops 4000000000 | bytes 3000000 | tf_op jit(solution)/shard_map/repack_attention/pallas_call | solution.py:393
  92.8 2.5 %finish.1 = (bf16[320,384]{1,0:T(8,128)(2,1)}, bf16[384,384]{1,0:T(8,128)(2,1)}, bf16[384,384]{1,0:T(8,128)(2,1)}, bf16[384,384]{1,0:T(8,128)(2,1)}) custom-call(bf16[320,384]{1,0:T(8,128)(2,1)} %get-tuple-element.9.att_in, bf16[384,384]{1,0:T(8,128)(2,1)} %get-tuple-element.10.dq_in, bf16[384,384]{1,0:T(8,128)(2,1)} %get-tuple-element.11.dv_in, ...), custom_call_target="tpu_custom_call" | custom-call | tf_op jit(solution)/shard_map/finish/pallas_call | solution.py:465

commit v5 on v4

--- a/solution.py
+++ b/solution.py
@@ -119,9 +119,9 @@
         pl.semaphore_signal(barrier, inc=1, device_id={"tensor": x_peer(i)}, device_id_type=MESH)
         return carry
 
-    lax.fori_loop(FAR, NZ - 1, greet_z, 0)
-    lax.fori_loop(0, NY - 1, greet_y, 0)
-    lax.fori_loop(0, TENSOR - 1, greet_x, 0)
+    lax.fori_loop(FAR, NZ - 1, greet_z, 0, unroll=True)
+    lax.fori_loop(0, NY - 1, greet_y, 0, unroll=True)
+    lax.fori_loop(0, TENSOR - 1, greet_x, 0, unroll=True)
 
     own_last = pltpu.make_async_copy(zsend.at[DK, z], last_hbm.at[z], own_sem)
     stores = [
@@ -372,13 +372,13 @@
     ]
     for load in loads:
         load.start()
+    for i in range(3):
+        loads[i + 2].wait()
+        stores[i].start()
     loads[0].wait()
     loads[1].wait()
     dk[...] = mm(unpack[...], last[...].reshape(SLOTS, COLS)).astype(BF)
     stores[3].start()
-    for i in range(3):
-        loads[i + 2].wait()
-        stores[i].start()
     for copy in stores:
         copy.wait()
 

time: 95.5 us -> 95.4 us (level)
  no operation moved by 1% of the time
where the time goes in v5:
time: 95.4 us; the launch traced here: 95.2 us
  Pallas kernels  94.5 us (99%)
    pallas_call x1, Pallas kernels, local(): pl.pallas_call(kernel, out_shape=(jax.ShapeDtypeStruct((PACK, COLS), BF),...  92.1 us
    pallas_call x1, Pallas kernels, local(): pl.pallas_call(finish, out_shape=(jax.ShapeDtypeStruct((PACK, COLS), BF),...  2.43 us

profile of v5, /device:TPU:1, one launch (start us, length us, event | category | flops | bytes accessed | tf_op | source)
XLA Modules:
  0.0 95.2 jit_solution(15206978434169411972)
XLA Ops:
  0.6 92.1 %repack_attention.1 = (bf16[320,384]{1,0:T(8,128)(2,1)}, bf16[384,384]{1,0:T(8,128)(2,1)}, bf16[384,384]{1,0:T(8,128)(2,1)}, bf16[16,24,384]{2,1,0:T(8,128)(2,1)}, bf16[384,384]{1,0:T(8,128)(2,1)}) custom-call(s32[384]{0:T(512)} %kept_hbm.1, s32[64]{0:T(128)} %dest_hbm.1, s32[64]{0:T(128)} %offset_hbm.1, s32[320]{0:T(512)} %image_hbm.1, ...), custom_call_target="tpu_custom_call" | custom-call | flops 4000000000 | bytes 3000000 | tf_op jit(solution)/shard_map/repack_attention/pallas_call | solution.py:393
  92.8 2.4 %finish.1 = (bf16[320,384]{1,0:T(8,128)(2,1)}, bf16[384,384]{1,0:T(8,128)(2,1)}, bf16[384,384]{1,0:T(8,128)(2,1)}, bf16[384,384]{1,0:T(8,128)(2,1)}) custom-call(bf16[320,384]{1,0:T(8,128)(2,1)} %get-tuple-element.9.att_in, bf16[384,384]{1,0:T(8,128)(2,1)} %get-tuple-element.10.dq_in, bf16[384,384]{1,0:T(8,128)(2,1)} %get-tuple-element.11.dv_in, ...), custom_call_target="tpu_custom_call" | custom-call | tf_op jit(solution)/shard_map/finish/pallas_call | solution.py:465
